TPU v7x, 128 devices: a whole 4x4x4 slice. The times are simulated.
128 devices in a mesh: role: 2 (over y_hi), dev: 64 (over z, x, y_lo, core).
Axes of the slice: x: 4, y: 4 (y_hi: 2, y_lo: 2; y = y_hi * 2 + y_lo), z: 4, core: 2. Of those that a mesh axis runs over, the one named last changes fastest.
Arguments:
- tokens: bfloat16 [65536, 1024], P(('role', 'dev')), may hold values from -6 to 6
- expert_ids: int32 [65536, 1], P(('role', 'dev')), may hold values from 0 to 127; in each aligned block of 512 rows (0 to 511, 512 to 1023, ...) at most 8 rows name the same one
- w_qkv: bfloat16 [1024, 3072], P(('role', 'dev')), may hold values from -2 to 2
- w_attn_out: bfloat16 [1024, 1024], P(('role', 'dev')), may hold values from -0.1875 to 0.1875
- gain_attn: bfloat16 [1024], replicated, may hold values from 0.5 to 1.5
- gain_expert: bfloat16 [1024], replicated, may hold values from 0.5 to 1.5
- router: bfloat16 [1024, 128], replicated, may hold values from -0.375 to 0.375
- expert_in: bfloat16 [128, 1024, 2816], P(('role', 'dev')), may hold values from -0.1875 to 0.1875
- expert_out: bfloat16 [128, 2816, 1024], P(('role', 'dev')), may hold values from -0.109375 to 0.109375
- capacity: int32 [128], replicated, may hold values from 256 to 1023
- swap_list: int32 [32], replicated, may hold values from 0 to 63, as said below
Outputs:
- mixed: bfloat16 [65536, 1024], P(('role', 'dev'))
Inputs may be any that keep to these rules, and one draw needn't show every extreme that they name: `expert_ids`: in the rows of one device no expert is named more than 8 times, a bound that some block reaches. `swap_list`: entries are distinct.
All inputs are finite; a program needn't handle non-finite values.
Results may differ from a plain program's by a relative error of at most 0.0052.
Values may be sent and summed in bfloat16 or wider, within the bound.
A program may use at most 128 MiB of HBM per device.

v0:
```python
import jax
import jax.numpy as jnp
from jax import lax
from jax.sharding import PartitionSpec as P

HEADS = 16


def rms_scale(values, gain_vector):
    mean_sq = jnp.mean(values * values, axis=-1, keepdims=True)
    return values * lax.rsqrt(mean_sq + 1e-06) * gain_vector.astype(jnp.float32)


def self_attend(qkv_rows, head_count):
    row_count = qkv_rows.shape[0]
    model_width = qkv_rows.shape[1] // 3
    head_size = model_width // head_count
    queries = qkv_rows[:, :model_width].reshape(row_count, head_count, head_size)
    keys_all = qkv_rows[:, model_width : 2 * model_width].reshape(row_count, head_count, head_size)
    values = qkv_rows[:, 2 * model_width :].reshape(row_count, head_count, head_size)
    scores = jnp.einsum(
        "shd,thd->hst", queries, keys_all, preferred_element_type=jnp.float32
    ) * head_size ** (-0.5)
    row_max = jnp.max(scores, axis=-1, keepdims=True)
    weights = jnp.exp(scores - row_max)
    soft_weights = (weights / jnp.sum(weights, axis=-1, keepdims=True)).astype(jnp.bfloat16)
    context = jnp.einsum("hst,thd->shd", soft_weights, values, preferred_element_type=jnp.float32)
    return context.reshape(row_count, model_width).astype(jnp.bfloat16)


def shards(
    tokens,
    expert_ids,
    w_qkv,
    w_attn_out,
    gain_attn,
    gain_expert,
    router,
    expert_in,
    expert_out,
    capacity,
    swap_list,
):
    seq_len, model_width = tokens.shape
    experts_all = router.shape[1]
    dev_count = lax.axis_size("dev")
    me = lax.axis_index("role") * dev_count + lax.axis_index("dev")
    chosen = expert_ids[:, 0]
    expert_range = jnp.arange(experts_all, dtype=jnp.int32)
    match = chosen[:, None] == expert_range[None, :]
    counts = jnp.sum(match.astype(jnp.float32), axis=0)
    row_share = w_attn_out.shape[0]
    beside = jnp.broadcast_to(counts.astype(jnp.bfloat16)[None, :], (row_share, experts_all))
    w_qkv_all = lax.all_gather(w_qkv, ("role", "dev"), axis=0, tiled=True)
    w_out_counts = lax.all_gather(
        jnp.concatenate([w_attn_out, beside], axis=1), ("role", "dev"), axis=0, tiled=True
    )
    w_out_all = w_out_counts[:, :model_width]
    counts_all = w_out_counts[:, model_width:].astype(jnp.float32)
    residual = tokens.astype(jnp.float32)
    normed = rms_scale(residual, gain_attn).astype(jnp.bfloat16)
    qkv_rows = jnp.dot(normed, w_qkv_all, preferred_element_type=jnp.float32).astype(jnp.bfloat16)
    context = self_attend(qkv_rows, HEADS)
    attended = jnp.dot(context, w_out_all, preferred_element_type=jnp.float32)
    hidden = residual + attended
    normed_ffn = rms_scale(hidden, gain_expert).astype(jnp.bfloat16)
    logits = jnp.dot(normed_ffn, router, preferred_element_type=jnp.float32)
    gate = jax.nn.sigmoid(jnp.sum(jnp.where(match, logits, 0.0), axis=1))
    gathered_row = jnp.arange(w_out_counts.shape[0], dtype=jnp.int32)
    first_of_lower = (gathered_row % row_share == 0) & (gathered_row < me * row_share)
    before = jnp.sum(jnp.where(first_of_lower[:, None], counts_all, 0.0), axis=0).astype(jnp.int32)
    row_ids = lax.broadcasted_iota(jnp.int32, (seq_len, seq_len), 0)
    col_ids = lax.broadcasted_iota(jnp.int32, (seq_len, seq_len), 1)
    strict_lower = (col_ids < row_ids).astype(jnp.bfloat16)
    rank_table = jnp.dot(
        strict_lower, match.astype(jnp.bfloat16), preferred_element_type=jnp.float32
    )
    local_rank = jnp.sum(jnp.where(match, rank_table, 0.0), axis=1).astype(jnp.int32)
    flagged = jnp.any(swap_list[:, None] == (expert_range % dev_count)[None, :], axis=0)
    location = jnp.where(
        flagged,
        (1 - expert_range // dev_count) * dev_count + expert_range % dev_count,
        expert_range,
    )
    cap_expert = jnp.sum(
        jnp.where(location[:, None] == expert_range[None, :], capacity[None, :], 0), axis=1
    )
    room = jnp.sum(jnp.where(match, (cap_expert - before)[None, :], 0), axis=1)
    kept = local_rank < room
    slot_rows = max(2, 2 * seq_len // experts_all)
    slot_index = chosen * slot_rows + local_rank
    buffer = (
        jnp.zeros((experts_all * slot_rows, model_width), jnp.bfloat16)
        .at[slot_index]
        .set(normed_ffn)
    )
    buffer = buffer.reshape(experts_all, slot_rows, model_width)
    received = lax.all_to_all(buffer, ("role", "dev"), split_axis=0, concat_axis=0, tiled=True)
    flat_rows = received.reshape(-1, model_width)
    activ = jnp.maximum(
        jnp.dot(flat_rows, expert_in[0], preferred_element_type=jnp.float32), 0.0
    ).astype(jnp.bfloat16)
    produced = jnp.dot(activ, expert_out[0], preferred_element_type=jnp.float32).astype(
        jnp.bfloat16
    )
    returned = lax.all_to_all(
        produced.reshape(received.shape), ("role", "dev"), split_axis=0, concat_axis=0, tiled=True
    )
    picked = returned.reshape(-1, model_width)[slot_index].astype(jnp.float32)
    mixed = hidden + jnp.where(kept, gate, 0.0)[:, None] * picked
    return mixed.astype(jnp.bfloat16)


def solution(mesh):
    return jax.shard_map(
        shards,
        mesh=mesh,
        in_specs=(
            P(("role", "dev"), None),
            P(("role", "dev"), None),
            P(("role", "dev"), None),
            P(("role", "dev"), None),
            P(),
            P(),
            P(),
            P(("role", "dev"), None, None),
            P(("role", "dev"), None, None),
            P(),
            P(),
        ),
        out_specs=P(("role", "dev"), None),
        check_vma=False,
    )
```

profile of v0, /device:TPU:1, one launch (start us, length us, event | category | flops | bytes accessed | tf_op | source)
XLA Modules:
  0.0 543.9 jit_solution(13328983588783734657)
XLA Ops:
  6.5 0.9 convert_reduce_fusion
  7.5 1.3 pad_maximum_fusion
  8.9 0.7 all-gather.3.cloned.1.call-update
  9.6 0.7 convert_element_type.81
  10.3 0.7 convert_element_type.93
  11.0 0.7 compare_reduce_fusion
  11.7 0.8 select_reduce_fusion.2
  12.5 1.1 fusion.30
  13.6 1.5 fusion.13
  15.1 192.9 %all-gather.5.cloned.1.call-done = bf16[1024,1152]{1,0:T(8,128)(2,1)} async-done(((bf16[8,1152]{1,0:T(8,128)(2,1)}), bf16[1024,1152]{1,0:T(8,128)(2,1)}) %all-gather.5.cloned.1.call-update) | async-done | bytes 2359312 | tf_op jit(solution)/shard_map/all_gather | solution.py:55
  208.1 1.2 select_reduce_fusion
  209.4 200.2 %all-gather.3.cloned.1.call-done = bf16[1024,3072]{1,0:T(8,128)(2,1)} async-done(((bf16[8,3072]{1,0:T(8,128)(2,1)}), bf16[1024,3072]{1,0:T(8,128)(2,1)}) %all-gather.3.cloned.1.call-update) | async-done | bytes 6291472 | tf_op jit(solution)/shard_map/all_gather | solution.py:54
  409.6 6.6 %convolution_convert_fusion = bf16[512,3072]{1,0:T(8,128)(2,1)S(1)} fusion(bf16[1024,3072]{1,0:T(8,128)(2,1)} %all-gather.3.cloned.1.call-done, bf16[512,1024]{1,0:T(8,128)(2,1)S(1)} %copy-done.2, f32[1024]{0:T(1024)S(1)} %convert_element_type.81, f32[512]{0:T(512)S(1)} %add_rsqrt_fusion.1), kind=kOutput, calls=%fused_computation.13 | convolution fusion | flops 3224895488 | bytes 10491904 | tf_op jit(solution)/shard_map/dot_general | solution.py:62
  416.5 1.3 copy.20
  418.9 8.9 %fusion.49 = (f32[16,512]{1,0:T(8,128)S(1)}, f32[16,512,512]{1,2,0:T(8,128)}) fusion(bf16[512,16,64]{0,2,1:T(8,128)(2,1)S(1)} %bitcast.42, bf16[512,16,64]{0,2,1:T(8,128)(2,1)S(1)} %bitcast.43), kind=kOutput, calls=%fused_computation.73 | convolution fusion | flops 549454336 | bytes 18907136 | tf_op jit(solution)/shard_map/sub | solution.py:25
  427.9 7.6 %fusion.28 = bf16[16,64,512]{2,1,0:T(8,128)(2,1)S(1)} fusion(bf16[512,16,64]{0,2,1:T(8,128)(2,1)S(1)} %bitcast.41, f32[16,512,512]{1,2,0:T(8,128)} %get-tuple-element.11, f32[16,512]{1,0:T(8,128)S(1)} %get-tuple-element.10), kind=kOutput, calls=%fused_computation.28 | convolution fusion | flops 545783808 | bytes 18907136 | tf_op jit(solution)/shard_map/hst,thd->shd/dot_general | solution.py:27
  435.5 1.4 multiply_reduce_fusion.1
  437.5 4.2 scatter_custom_fusion
  441.7 37.2 %all_to_all.10 = bf16[128,8,1024]{2,1,0:T(8,128)(2,1)S(1)} all-to-all(bf16[128,8,1024]{2,1,0:T(8,128)(2,1)} %bitcast.40), channel_id=1, replica_groups=mesh['role'=2,'dev'=64] {'role','dev'}, dimensions={0} | all-to-all | bytes 4194304 | tf_op jit(solution)/shard_map/all_to_all | solution.py:98
  478.9 17.7 %convert_bitcast_fusion = bf16[128,8,1024]{2,1,0:T(8,128)(2,1)} fusion(bf16[1,2816,1024]{2,1,0:T(8,128)(2,1)} %param.19, bf16[1,1024,2816]{2,1,0:T(8,128)(2,1)} %param.18, bf16[128,8,1024]{2,1,0:T(8,128)(2,1)S(1)} %all_to_all.10), kind=kOutput, calls=%fused_computation.25 | convolution fusion | flops 11817975808 | bytes 15728640 | tf_op jit(solution)/shard_map/dot_general | solution.py:103
  496.6 5.4 all-to-all-start.1
  502.0 30.1 %all-to-all-done.1 = bf16[128,8,1024]{2,1,0:T(8,128)(2,1)S(1)} async-done(((bf16[128,8,1024]{2,1,0:T(8,128)(2,1)}), bf16[128,8,1024]{2,1,0:T(8,128)(2,1)S(1)}, u32[]{:S(2)}, u32[]{:S(2)}) %all-to-all-start.1) | async-done | bytes 2097184 | tf_op jit(solution)/shard_map/all_to_all | solution.py:106
  532.1 2.0 gather_fusion
  534.2 2.9 add_convert_fusion
  (32 shorter events, 2.3 us)
Async XLA Ops:
  6.5 430.3 %copy-start = (bf16[1024,128]{1,0:T(8,128)(2,1)S(1)}, bf16[1024,128]{1,0:T(8,128)(2,1)}, u32[]{:S(2)}) copy-start(bf16[1024,128]{1,0:T(8,128)(2,1)} %param.17) | copy-start | bytes 786436
  6.5 202.7 %copy-start.5 = (s32[512,1]{0,1:T(1,128)S(1)}, s32[512,1]{0,1:T(1,128)}, u32[]{:S(2)}) copy-start(s32[512,1]{0,1:T(1,128)} %param.12) | copy-start | bytes 6148
  6.5 403.0 %copy-start.2 = (bf16[512,1024]{1,0:T(8,128)(2,1)S(1)}, bf16[512,1024]{1,0:T(8,128)(2,1)}, u32[]{:S(2)}) copy-start(bf16[512,1024]{1,0:T(8,128)(2,1)} %param.11) | copy-start | bytes 3145732
  6.5 201.5 %all-gather.5.cloned.1.call-start = ((), (), s32[]{:S(2)}) async-start(), calls=%async_computation.3 | async-start | bytes 2377728 | tf_op jit(solution)/shard_map/all_gather | solution.py:55
  8.8 400.8 %all-gather.3.cloned.1.call-start = ((), (), s32[]{:S(2)}) async-start(), calls=%async_computation.2 | async-start | bytes 6340608 | tf_op jit(solution)/shard_map/all_gather | solution.py:54
  418.9 8.9 %copy-start.4 = (bf16[512,1024]{0,1:T(8,128)(2,1)S(1)}, bf16[512,1024]{0,1:T(8,128)(2,1)}, u32[]{:S(2)}) copy-start(bf16[512,1024]{0,1:T(8,128)(2,1)} %copy.20) | copy-start | bytes 3145732
  427.8 7.6 %copy-start.3 = (bf16[512,1024]{1,0:T(8,128)(2,1)S(1)}, bf16[512,1024]{1,0:T(8,128)(2,1)}, u32[]{:S(2)}) copy-start(bf16[512,1024]{1,0:T(8,128)(2,1)} %param.11) | copy-start | bytes 3145732
  427.9 7.6 %copy-start.6 = (bf16[1024,1152]{1,0:T(8,128)(2,1)S(1)}, bf16[1024,1152]{1,0:T(8,128)(2,1)}, u32[]{:S(2)}) copy-start(bf16[1024,1152]{1,0:T(8,128)(2,1)} %all-gather.5.cloned.1.call-done) | copy-start | bytes 7077892
  436.8 4.9 copy-start.1
  496.6 35.6 %all-to-all-start.1 = ((bf16[128,8,1024]{2,1,0:T(8,128)(2,1)}), bf16[128,8,1024]{2,1,0:T(8,128)(2,1)S(1)}, u32[]{:S(2)}, u32[]{:S(2)}) async-start(bf16[128,8,1024]{2,1,0:T(8,128)(2,1)} %convert_bitcast_fusion), calls=%async_computation.1 | async-start | bytes 4194304 | tf_op jit(solution)/shard_map/all_to_all | solution.py:106
Sparse Core Ops, SparseCore 0:
  9.1 198.9 all-gather.4
  209.8 199.7 all-gather.2
where the time goes:
time: 544 us
  waiting for transfers between devices  424 us (78%)
  matrix products  43.8 us (8%)
  blocking collectives  37.2 us (7%)
  other arithmetic  15.1 us (3%)
  between operations  13.6 us (2%)
  starting transfers between devices  5.47 us (1%)
    all_gather x1, waiting for transfers between devices, shards(): w_qkv_all = lax.all_gather(w_qkv, ('role', 'dev'), axis=0, tiled=True)  200 us
    all_gather x1, waiting for transfers between devices, shards(): lax.all_gather(jnp.concatenate([w_attn_out, beside], axis=1), ('role', 'd...  193 us
    all_to_all x1, blocking collectives, shards(): lax.all_to_all(buffer, ('role', 'dev'), split_axis=0, concat_axis=0, tile...  37.2 us
    all_to_all x1, waiting for transfers between devices, shards(): lax.all_to_all(produced.reshape(received.shape), ('role', 'dev'), split_a...  30.1 us
    dot_general x1, matrix products, shards(): jnp.dot(activ, expert_out[0], preferred_element_type=jnp.float32)  17.7 us
  transfers between devices with their start and end apart: 3, of which 3 were waited for; matrix products, arithmetic and copies ran while one was open for 1% of the time, Pallas kernels for 0%

commit v1 on v0

--- a/solution.py
+++ b/solution.py
@@ -4,6 +4,11 @@
 from jax.sharding import PartitionSpec as P
 
 HEADS = 16
+
+
+def swapped_in(x, axis, along):
+    sent = jnp.stack([x] * lax.axis_size(axis))
+    return jnp.concatenate(lax.all_to_all(sent, axis, 0, 0), axis=along)
 
 
 def rms_scale(values, gain_vector):
@@ -52,9 +57,7 @@
     row_share = w_attn_out.shape[0]
     beside = jnp.broadcast_to(counts.astype(jnp.bfloat16)[None, :], (row_share, experts_all))
     w_qkv_all = lax.all_gather(w_qkv, ("role", "dev"), axis=0, tiled=True)
-    w_out_counts = lax.all_gather(
-        jnp.concatenate([w_attn_out, beside], axis=1), ("role", "dev"), axis=0, tiled=True
-    )
+    w_out_counts = swapped_in(jnp.concatenate([w_attn_out, beside], axis=1), ("role", "dev"), 0)
     w_out_all = w_out_counts[:, :model_width]
     counts_all = w_out_counts[:, model_width:].astype(jnp.float32)
     residual = tokens.astype(jnp.float32)

time: 544 us -> 367 us (0.67)
  waiting for transfers between devices: 424 us -> 238 us
  starting transfers between devices: 5.47 us -> 16.9 us
    all_gather x1 -> x0, waiting for transfers between devices: 193 us -> none  [shards(): lax.all_gather(jnp.concatenate([w_attn_out, beside], axis=1), ('role', 'd...]
    all_to_all x0 -> x1, waiting for transfers between devices: none -> 31.1 us  [swapped_in(): return jnp.concatenate(lax.all_to_all(sent, axis, 0, 0), axis=along)]
    all_gather x1, waiting for transfers between devices: 200 us -> 176 us  [shards(): w_qkv_all = lax.all_gather(w_qkv, ('role', 'dev'), axis=0, tiled=True)]
    all_to_all x0 -> x1, starting transfers between devices: none -> 11.5 us  [swapped_in(): return jnp.concatenate(lax.all_to_all(sent, axis, 0, 0), axis=along)]
  transfers between devices with their start and end apart: 3 -> 3, of which waited for: 3 -> 3; matrix products, arithmetic and copies ran while one was open for 1% -> 2% of each run, Pallas kernels for 0% -> 0%
where the time goes in v1:
time: 367 us; the launch traced here: 366 us
  waiting for transfers between devices  238 us (65%)
  matrix products  43 us (12%)
  blocking collectives  37.8 us (10%)
  starting transfers between devices  16.9 us (5%)
  between operations  13.6 us (4%)
  other arithmetic  10.8 us (3%)
  local copies, waits for them, and re-layouts  6.43 us (2%)
    all_gather x1, waiting for transfers between devices, shards(): w_qkv_all = lax.all_gather(w_qkv, ('role', 'dev'), axis=0, tiled=True)  176 us
    all_to_all x1, blocking collectives, shards(): lax.all_to_all(buffer, ('role', 'dev'), split_axis=0, concat_axis=0, tile...  37.8 us
    all_to_all x1, waiting for transfers between devices, swapped_in(): return jnp.concatenate(lax.all_to_all(sent, axis, 0, 0), axis=along)  31.1 us
    all_to_all x1, waiting for transfers between devices, shards(): lax.all_to_all(produced.reshape(received.shape), ('role', 'dev'), split_a...  30.1 us
    dot_general x1, matrix products, shards(): jnp.dot(activ, expert_out[0], preferred_element_type=jnp.float32)  17.7 us
    all_to_all x1, starting transfers between devices, swapped_in(): return jnp.concatenate(lax.all_to_all(sent, axis, 0, 0), axis=along)  11.5 us
    sub x1, matrix products, self_attend(): weights = jnp.exp(scores - row_max)  8.9 us
    dot_general x1, matrix products, self_attend(): jnp.einsum('hst,thd->shd', soft_weights, values, preferred_element_type=j...  7.5 us
  transfers between devices with their start and end apart: 3, of which 3 were waited for; matrix products, arithmetic and copies ran while one was open for 2% of the time, Pallas kernels for 0%

profile of v1, /device:TPU:1, one launch (start us, length us, event | category | flops | bytes accessed | tf_op | source)
XLA Modules:
  0.0 366.2 jit_solution(9466304198877491365)
XLA Ops:
  6.5 0.7 all-gather.2.cloned.1.call-update
  7.3 0.8 convert_reduce_fusion
  8.1 0.7 pad_maximum_fusion
  8.8 1.6 stack.2
  10.4 11.5 %all-to-all-start = ((bf16[128,8,1152]{2,1,0:T(8,128)(2,1)}), bf16[128,8,1152]{2,1,0:T(8,128)(2,1)S(1)}, u32[]{:S(2)}, u32[]{:S(2)}) async-start(bf16[128,8,1152]{2,1,0:T(8,128)(2,1)} %stack.2), calls=%async_computation | async-start | bytes 4718592 | tf_op jit(solution)/shard_map/all_to_all | solution.py:11
  22.6 1.5 fusion.13
  24.1 31.1 %all-to-all-done = bf16[128,8,1152]{2,1,0:T(8,128)(2,1)S(1)} async-done(((bf16[128,8,1152]{2,1,0:T(8,128)(2,1)}), bf16[128,8,1152]{2,1,0:T(8,128)(2,1)S(1)}, u32[]{:S(2)}, u32[]{:S(2)}) %all-to-all-start) | async-done | bytes 2359328 | tf_op jit(solution)/shard_map/all_to_all | solution.py:11
  55.6 175.7 %all-gather.2.cloned.1.call-done = bf16[1024,3072]{1,0:T(8,128)(2,1)} async-done(((bf16[8,3072]{1,0:T(8,128)(2,1)}), bf16[1024,3072]{1,0:T(8,128)(2,1)}) %all-gather.2.cloned.1.call-update) | async-done | bytes 6291472 | tf_op jit(solution)/shard_map/all_gather | solution.py:59
  231.4 6.6 %convolution_convert_fusion = bf16[512,3072]{1,0:T(8,128)(2,1)S(1)} fusion(bf16[1024,3072]{1,0:T(8,128)(2,1)} %all-gather.2.cloned.1.call-done, bf16[512,1024]{1,0:T(8,128)(2,1)} %param.11, f32[1024]{0:T(1024)S(1)} %convert_element_type.81, f32[512]{0:T(512)S(1)} %add_rsqrt_fusion.1), kind=kOutput, calls=%fused_computation.13 | convolution fusion | flops 3224895488 | bytes 10491904 | tf_op jit(solution)/shard_map/dot_general | solution.py:65
  238.0 0.3 fusion.48
  238.3 1.3 copy.20
  239.7 0.5 copy.21
  240.2 0.5 copy.22
  240.8 8.9 %fusion.49 = (f32[16,512]{1,0:T(8,128)S(1)}, f32[16,512,512]{1,2,0:T(8,128)}) fusion(bf16[512,16,64]{0,2,1:T(8,128)(2,1)S(1)} %bitcast.45, bf16[512,16,64]{0,2,1:T(8,128)(2,1)S(1)} %bitcast.46), kind=kOutput, calls=%fused_computation.73 | convolution fusion | flops 549454336 | bytes 18907136 | tf_op jit(solution)/shard_map/sub | solution.py:30
  249.7 7.5 %fusion.28 = bf16[16,64,512]{2,1,0:T(8,128)(2,1)S(1)} fusion(bf16[512,16,64]{0,2,1:T(8,128)(2,1)S(1)} %bitcast.44, f32[16,512,512]{1,2,0:T(8,128)} %get-tuple-element.11, f32[16,512]{1,0:T(8,128)S(1)} %get-tuple-element.10), kind=kOutput, calls=%fused_computation.28 | convolution fusion | flops 545783808 | bytes 18907136 | tf_op jit(solution)/shard_map/hst,thd->shd/dot_general | solution.py:32
  257.2 1.4 multiply_reduce_fusion.1
  258.6 0.6 fusion.29
  259.2 4.2 %scatter_custom_fusion = bf16[1024,1024]{1,0:T(8,128)(2,1)} fusion(s32[512]{0:T(512)S(1)} %bitcast.51, bf16[]{:T(256)} %constant.86.clone.1, f32[512,1024]{1,0:T(8,128)S(1)} %get-tuple-element.13, f32[1024]{0:T(1024)S(1)} %convert_element_type.93, f32[512]{0:T(512)S(1)} %add_rsqrt_fusion), kind=kCustom, calls=%fused_computation.33 | custom fusion | flops 1572864 | bytes 4200450 | tf_op jit(solution)/shard_map/scatter | solution.py:98
  263.4 37.8 %all_to_all.15 = bf16[128,8,1024]{2,1,0:T(8,128)(2,1)S(1)} all-to-all(bf16[128,8,1024]{2,1,0:T(8,128)(2,1)} %bitcast.41), channel_id=1, replica_groups=mesh['role'=2,'dev'=64] {'role','dev'}, dimensions={0} | all-to-all | bytes 4194304 | tf_op jit(solution)/shard_map/all_to_all | solution.py:101
  301.2 17.7 %convert_bitcast_fusion = bf16[128,8,1024]{2,1,0:T(8,128)(2,1)} fusion(bf16[1,2816,1024]{2,1,0:T(8,128)(2,1)} %param.19, bf16[1,1024,2816]{2,1,0:T(8,128)(2,1)} %param.18, bf16[128,8,1024]{2,1,0:T(8,128)(2,1)S(1)} %all_to_all.15), kind=kOutput, calls=%fused_computation.25 | convolution fusion | flops 11817975808 | bytes 15728640 | tf_op jit(solution)/shard_map/dot_general | solution.py:106
  318.9 5.4 %all-to-all-start.2 = ((bf16[128,8,1024]{2,1,0:T(8,128)(2,1)}), bf16[128,8,1024]{2,1,0:T(8,128)(2,1)S(1)}, u32[]{:S(2)}, u32[]{:S(2)}) async-start(bf16[128,8,1024]{2,1,0:T(8,128)(2,1)} %convert_bitcast_fusion), calls=%async_computation.2 | async-start | bytes 4194304 | tf_op jit(solution)/shard_map/all_to_all | solution.py:109
  324.3 30.1 %all-to-all-done.2 = bf16[128,8,1024]{2,1,0:T(8,128)(2,1)S(1)} async-done(((bf16[128,8,1024]{2,1,0:T(8,128)(2,1)}), bf16[128,8,1024]{2,1,0:T(8,128)(2,1)S(1)}, u32[]{:S(2)}, u32[]{:S(2)}) %all-to-all-start.2) | async-done | bytes 2097184 | tf_op jit(solution)/shard_map/all_to_all | solution.py:109
  354.4 2.0 gather_fusion
  356.5 2.9 add_convert_fusion
  (40 shorter events, 1.0 us)
Async XLA Ops:
  6.5 252.1 %copy-start = (bf16[1024,128]{1,0:T(8,128)(2,1)S(1)}, bf16[1024,128]{1,0:T(8,128)(2,1)}, u32[]{:S(2)}) copy-start(bf16[1024,128]{1,0:T(8,128)(2,1)} %param.17) | copy-start | bytes 786436
  6.5 224.8 %all-gather.2.cloned.1.call-start = ((), (), s32[]{:S(2)}) async-start(), calls=%async_computation.3 | async-start | bytes 6340608 | tf_op jit(solution)/shard_map/all_gather | solution.py:59
  10.4 11.5 %copy-start.7 = (bf16[1024]{0:T(1024)(128)(2,1)S(1)}, bf16[1024]{0:T(1024)(128)(2,1)}, u32[]{:S(2)}) copy-start(bf16[1024]{0:T(1024)(128)(2,1)} %param.15) | copy-start | bytes 6148
  10.4 11.6 %copy-start.8 = (bf16[1024]{0:T(1024)(128)(2,1)S(1)}, bf16[1024]{0:T(1024)(128)(2,1)}, u32[]{:S(2)}) copy-start(bf16[1024]{0:T(1024)(128)(2,1)} %param.16) | copy-start | bytes 6148
  10.4 11.6 %copy-start.9 = (s32[32]{0:T(128)S(1)}, s32[32]{0:T(128)}, u32[]{:S(2)}) copy-start(s32[32]{0:T(128)} %param.21) | copy-start | bytes 388
  10.4 11.7 %copy-start.10 = (s32[128]{0:T(128)S(1)}, s32[128]{0:T(128)}, u32[]{:S(2)}) copy-start(s32[128]{0:T(128)} %param.20) | copy-start | bytes 1540
  10.4 11.9 %copy-start.6 = (s32[512,1]{0,1:T(1,128)S(1)}, s32[512,1]{0,1:T(1,128)}, u32[]{:S(2)}) copy-start(s32[512,1]{0,1:T(1,128)} %param.12) | copy-start | bytes 6148
  10.4 44.9 %all-to-all-start = ((bf16[128,8,1152]{2,1,0:T(8,128)(2,1)}), bf16[128,8,1152]{2,1,0:T(8,128)(2,1)S(1)}, u32[]{:S(2)}, u32[]{:S(2)}) async-start(bf16[128,8,1152]{2,1,0:T(8,128)(2,1)} %stack.2), calls=%async_computation | async-start | bytes 4718592 | tf_op jit(solution)/shard_map/all_to_all | solution.py:11
  55.3 176.1 %copy-start.2 = (bf16[128,8,1152]{2,1,0:T(8,128)(2,1)}, bf16[128,8,1152]{2,1,0:T(8,128)(2,1)S(1)}, u32[]{:S(2)}) copy-start(bf16[128,8,1152]{2,1,0:T(8,128)(2,1)S(1)} %all-to-all-done) | copy-start | bytes 7077892
  240.8 8.9 %copy-start.5 = (bf16[512,1024]{0,1:T(8,128)(2,1)S(1)}, bf16[512,1024]{0,1:T(8,128)(2,1)}, u32[]{:S(2)}) copy-start(bf16[512,1024]{0,1:T(8,128)(2,1)} %copy.20) | copy-start | bytes 3145732
  249.7 7.5 %copy-start.3 = (bf16[128,8,1152]{2,1,0:T(8,128)(2,1)S(1)}, bf16[128,8,1152]{2,1,0:T(8,128)(2,1)}, u32[]{:S(2)}) copy-start(bf16[128,8,1152]{2,1,0:T(8,128)(2,1)} %copy-done.2) | copy-start | bytes 7077892
  249.7 7.5 %copy-start.4 = (bf16[512,1024]{1,0:T(8,128)(2,1)S(1)}, bf16[512,1024]{1,0:T(8,128)(2,1)}, u32[]{:S(2)}) copy-start(bf16[512,1024]{1,0:T(8,128)(2,1)} %param.11) | copy-start | bytes 3145732
  258.6 4.8 %copy-start.1 = (f32[512,1024]{1,0:T(8,128)}, f32[512,1024]{1,0:T(8,128)S(1)}, u32[]{:S(2)}) copy-start(f32[512,1024]{1,0:T(8,128)S(1)} %get-tuple-element.13) | copy-start | bytes 6291460
  318.9 35.6 %all-to-all-start.2 = ((bf16[128,8,1024]{2,1,0:T(8,128)(2,1)}), bf16[128,8,1024]{2,1,0:T(8,128)(2,1)S(1)}, u32[]{:S(2)}, u32[]{:S(2)}) async-start(bf16[128,8,1024]{2,1,0:T(8,128)(2,1)} %convert_bitcast_fusion), calls=%async_computation.2 | async-start | bytes 4194304 | tf_op jit(solution)/shard_map/all_to_all | solution.py:109
Sparse Core Ops, SparseCore 0:
  9.1 222.2 all-gather.1
